TPU v7x, 32 devices: a whole 2x2x4 slice. The times are simulated.
32 devices in a mesh: row: 8 (over z, x), col: 4 (over y, core).
Axes of the slice: x: 2, y: 2, z: 4, core: 2. Of those that a mesh axis runs over, the one named last changes fastest.
Arguments:
- hidden: bfloat16 [8192, 1600], P('row', 'col'), may hold values from -60 to 60
- up_weight: bfloat16 [1600, 6400], P('row', 'col'), may hold values from -0.15625 to 0.15625
- up_bias: float32 [6400], P('col'), may hold values from -3 to 3
- down_weight: bfloat16 [6400, 1600], P('col', 'row'), may hold values from -0.078125 to 0.078125
- down_bias: float32 [1600], P('col'), may hold values from -3 to 3
- query_key_value_weight: bfloat16 [1600, 4800], P('row', 'col'), may hold values from -0.15625 to 0.15625
- query_key_value_bias: float32 [4800], P('col'), may hold values from -3 to 3
- block_norm_gain: float32 [1600], replicated, may hold values from 0.1 to 1.9
- block_norm_shift: float32 [1600], replicated, may hold values from -3 to 3
- following_norm_gain: float32 [1600], replicated, may hold values from 0.1 to 1.9
- following_norm_shift: float32 [1600], replicated, may hold values from -3 to 3
- up_down_factors: bfloat16 [32, 16, 1600], P('row'), may hold values from -0.15625 to 0.15625
- up_up_factors: bfloat16 [32, 16, 6400], P('row', None, 'col'), may hold values from -1.5 to 1.5
- query_key_value_down_factors: bfloat16 [32, 16, 1600], P('row'), may hold values from -0.15625 to 0.15625
- query_key_value_up_factors: bfloat16 [32, 16, 4800], P('row', None, 'col'), may hold values from -1.5 to 1.5
- adapter_storage_slot: int32 [32], replicated, may hold values from 0 to 31, as said below
- tile_adapter_index: int32 [64], P('row'), may hold values from 0 to 31, as said below
- tile_token_rows: int32 [64], P('row'), may hold values from 1 to 128, as said below
Outputs:
- h_out: bfloat16 [8192, 1600], P('row', 'col')
- qkv: bfloat16 [8192, 4800], P('row', 'col')
Inputs may be any that keep to these rules, and one draw needn't show every extreme that they name: A permutation: adapter a is stored in slot adapter_storage_slot[a], and index r of row holds slots r * 4 to (r + 1) * 4 - 1. `tile_adapter_index`: the 8 tiles of one index of row name adapters whose slots lie on distinct indices of row. A tile's first tile_token_rows rows are prompt tokens, the rest padding.
All inputs are finite; a program needn't handle non-finite values.
Results may differ from a plain program's by a relative error of at most 0.02.
Values may be sent and summed in bfloat16 or wider, within the bound.
A program may use at most 64 MiB of HBM per device.

v0:
```python
import jax
import jax.numpy as jnp
from jax import lax
from jax.sharding import PartitionSpec as P


def layer_norm(values, gain_vec, shift_vec):
    row_mean = jnp.mean(values, axis=-1, keepdims=True)
    centred = values - row_mean
    variance = jnp.mean(centred * centred, axis=-1, keepdims=True)
    return centred * lax.rsqrt(variance + 1e-05) * gain_vec + shift_vec


def fold_rows(operand, weight_piece):
    return jnp.dot(operand, weight_piece, preferred_element_type=jnp.float32)


def adapter_update(
    normalized_input, down_factor, up_factor, holder_row, resident_slot, tile_total_count
):
    tok_rows, feat_width = normalized_input.shape
    tile_len = tok_rows // tile_total_count
    per_holder, adapter_rank_size, unused_result = down_factor.shape
    tiled_rows = normalized_input.reshape(tile_total_count, tile_len, feat_width)
    owners = lax.axis_size("row")
    select = (holder_row[None, :] == jnp.arange(owners, dtype=jnp.int32)[:, None]).astype(
        jnp.bfloat16
    )
    slot_pick = (resident_slot[:, None] == jnp.arange(per_holder, dtype=jnp.int32)[None, :]).astype(
        jnp.bfloat16
    )
    outgoing = jnp.einsum(
        "ot,tid->oid", select, tiled_rows, preferred_element_type=jnp.float32
    ).astype(jnp.bfloat16)
    labels = jnp.dot(select, slot_pick, preferred_element_type=jnp.float32).astype(jnp.bfloat16)
    received_rows, slot_marks = (
        lax.all_to_all(outgoing, "row", split_axis=0, concat_axis=0, tiled=True),
        lax.all_to_all(labels, "row", split_axis=0, concat_axis=0, tiled=True),
    )
    every_low_rank = jnp.einsum(
        "kph,fch->kpfc", received_rows, down_factor, preferred_element_type=jnp.float32
    )
    low_rank = jnp.sum(
        every_low_rank * slot_marks.astype(jnp.float32)[:, None, :, None], axis=2
    ).astype(jnp.bfloat16)
    broadcast_rows = (low_rank[:, :, None, :] * slot_marks[:, None, :, None]).reshape(
        owners, tile_len, per_holder * adapter_rank_size
    )
    answer = jnp.einsum(
        "sik,kf->sif",
        broadcast_rows,
        up_factor.reshape(per_holder * adapter_rank_size, -1),
        preferred_element_type=jnp.float32,
    ).astype(jnp.bfloat16)
    returned = lax.all_to_all(answer, "row", split_axis=0, concat_axis=0, tiled=True)
    update_rows = jnp.einsum(
        "ot,oif->tif", select, returned, preferred_element_type=jnp.float32
    ).astype(jnp.bfloat16)
    update_rows = lax.optimization_barrier(update_rows)
    return update_rows.reshape(tok_rows, -1).astype(jnp.float32)


def per_device(
    hidden,
    up_weight,
    up_bias,
    down_weight,
    down_bias,
    query_key_value_weight,
    query_key_value_bias,
    block_norm_gain,
    block_norm_shift,
    following_norm_gain,
    following_norm_shift,
    up_down_factors,
    up_up_factors,
    query_key_value_down_factors,
    query_key_value_up_factors,
    adapter_storage_slot,
    tile_adapter_index,
    tile_token_rows,
):
    tok_rows = hidden.shape[0]
    tile_total_count = tile_adapter_index.shape[0]
    tile_len = tok_rows // tile_total_count
    per_holder = up_down_factors.shape[0]
    adapter_count = adapter_storage_slot.shape[0]
    adapter_pick = (
        tile_adapter_index[:, None] == jnp.arange(adapter_count, dtype=jnp.int32)[None, :]
    ).astype(jnp.int32)
    slot_ids = jnp.sum(adapter_pick * adapter_storage_slot[None, :], axis=1)
    holder_row = slot_ids // per_holder
    resident_slot = slot_ids % per_holder
    valid = (jnp.arange(tile_len, dtype=jnp.int32)[None, :] < tile_token_rows[:, None]).reshape(
        tok_rows, 1
    )
    gathered = lax.all_gather(hidden, "col", axis=1, tiled=True)
    normalized_input = layer_norm(
        gathered.astype(jnp.float32), block_norm_gain, block_norm_shift
    ).astype(jnp.bfloat16)
    up_dense = fold_rows(normalized_input, lax.all_gather(up_weight, "row", axis=0, tiled=True))
    up_projection = (
        up_dense
        + up_bias
        + adapter_update(
            normalized_input,
            up_down_factors,
            up_up_factors,
            holder_row,
            resident_slot,
            tile_total_count,
        )
    )
    activated = jax.nn.gelu(up_projection, approximate=True).astype(jnp.bfloat16)
    partial_value = jnp.dot(
        activated,
        lax.all_gather(down_weight, "row", axis=1, tiled=True),
        preferred_element_type=jnp.float32,
    )
    summed = lax.psum_scatter(
        partial_value.astype(jnp.bfloat16), "col", scatter_dimension=1, tiled=True
    ).astype(jnp.float32)
    mixed = hidden.astype(jnp.float32) + summed + down_bias
    h_out = jnp.where(valid, mixed, 0.0).astype(jnp.bfloat16)
    gathered_next = lax.all_gather(h_out, "col", axis=1, tiled=True)
    normalized_following = layer_norm(
        gathered_next.astype(jnp.float32), following_norm_gain, following_norm_shift
    ).astype(jnp.bfloat16)
    qkv_dense = fold_rows(
        normalized_following, lax.all_gather(query_key_value_weight, "row", axis=0, tiled=True)
    )
    projected_output = (
        qkv_dense
        + query_key_value_bias
        + adapter_update(
            normalized_following,
            query_key_value_down_factors,
            query_key_value_up_factors,
            holder_row,
            resident_slot,
            tile_total_count,
        )
    )
    qkv = jnp.where(valid, projected_output, 0.0).astype(jnp.bfloat16)
    return (h_out, qkv)


def solution(mesh):
    in_specs = (
        P("row", "col"),
        P("row", "col"),
        P("col"),
        P("col", "row"),
        P("col"),
        P("row", "col"),
        P("col"),
        P(),
        P(),
        P(),
        P(),
        P("row", None, None),
        P("row", None, "col"),
        P("row", None, None),
        P("row", None, "col"),
        P(),
        P("row"),
        P("row"),
    )
    out_specs = (P("row", "col"), P("row", "col"))
    return jax.shard_map(
        per_device, mesh=mesh, in_specs=in_specs, out_specs=out_specs, check_vma=False
    )
```

profile of v0, /device:TPU:0, one launch (start us, length us, event | category | flops | bytes accessed | tf_op | source)
XLA Modules:
  0.0 654.0 jit_solution(14058357577489934825)
XLA Ops:
  10.5 7.3 %all-to-all-start.1 = ((bf16[8,1,4]{2,1,0:T(2,128)(2,1)}), bf16[8,1,4]{2,1,0:T(2,128)(2,1)S(1)}, u32[]{:S(2)}, u32[]{:S(2)}) async-start(bf16[8,1,4]{2,1,0:T(2,128)(2,1)} %copy.30), calls=%async_computation.1 | async-start | bytes 8192 | tf_op jit(solution)/shard_map/all_to_all | solution.py:38
  17.8 23.9 %all-gather.6.cloned.1.call-done = bf16[1024,1600]{0,1:T(8,128)(2,1)} async-done(((bf16[1024,400]{0,1:T(8,128)(2,1)}), bf16[1024,1600]{0,1:T(8,128)(2,1)}) %all-gather.6.cloned.1.call-update) | async-done | bytes 3276816 | tf_op jit(solution)/shard_map/all_gather | solution.py:97
  41.6 2.7 convert_reduce_fusion.1
  49.4 2.3 copy.29
  51.7 5.5 all-to-all-start
  58.2 127.9 %all-to-all-done = bf16[8,128,1600]{1,2,0:T(8,128)(2,1)} async-done(((bf16[8,128,1600]{1,2,0:T(8,128)(2,1)}), bf16[8,128,1600]{1,2,0:T(8,128)(2,1)}, u32[]{:S(2)}, u32[]{:S(2)}) %all-to-all-start) | async-done | bytes 3276832 | tf_op jit(solution)/shard_map/all_to_all | solution.py:37
  186.1 2.6 fusion.45
  189.9 138.7 %all_to_all.33 = bf16[8,128,1600]{1,2,0:T(8,128)(2,1)S(1)} all-to-all(bf16[8,128,1600]{1,2,0:T(8,128)(2,1)S(1)} %bitcast_convert_fusion), channel_id=1, replica_groups=mesh['row'=8,'col'=4] {'row'}, dimensions={0} | all-to-all | bytes 6553600 | tf_op jit(solution)/shard_map/all_to_all | solution.py:55
  328.5 2.0 fusion.30
  330.6 2.9 convert_element_type.115
  333.5 14.9 %fusion.19.clone.4 = bf16[1024,1600]{0,1:T(8,128)(2,1)} fusion(f32[200,8,8,128]{3,2,1,0:T(8,128)} %bitcast.93, bf16[1600,1600]{1,0:T(8,128)(2,1)} %all-gather.8.cloned.1.call-done, f32[1600]{0:T(1024)S(1)} %copy-done.11, bf16[1024,1600]{0,1:T(8,128)(2,1)S(1)} %copy-done.2, f32[1600]{0:T(1024)S(1)} %copy-done.6, f32[1600]{0:T(1024)S(1)} %copy-done.7, ...), kind=kOutput, calls=%fused_computation.24.clone.clone.clone.1 | convolution fusion | flops 5270732800 | bytes 18254592 | tf_op jit(solution)/shard_map/dot_general | solution.py:15
  348.4 10.8 %convolution_convert_fusion = bf16[1024,1600]{0,1:T(8,128)(2,1)} fusion(bf16[1600,1600]{0,1:T(8,128)(2,1)} %all-gather.10.cloned.1.call-done, bf16[1024,1600]{0,1:T(8,128)(2,1)} %fusion.19.clone.4), kind=kOutput, calls=%fused_computation.31 | convolution fusion | flops 5244518400 | bytes 11673600 | tf_op jit(solution)/shard_map/dot_general | solution.py:115
  359.4 38.2 %reduce-scatter.2.cloned.1.call-done = bf16[1024,400]{0,1:T(8,128)(2,1)} async-done(((bf16[1024,1600]{0,1:T(8,128)(2,1)}), bf16[1024,400]{0,1:T(8,128)(2,1)}) %reduce-scatter.2.cloned.1.call-update) | async-done | bytes 819216 | tf_op jit(solution)/shard_map/reduce_scatter | solution.py:120
  397.7 2.3 select_convert_fusion
  400.0 29.4 %all-gather.12.cloned.1.call-done = bf16[1024,1600]{0,1:T(8,128)(2,1)} async-done(((bf16[1024,400]{0,1:T(8,128)(2,1)}), bf16[1024,1600]{0,1:T(8,128)(2,1)}) %all-gather.12.cloned.1.call-update) | async-done | bytes 3276816 | tf_op jit(solution)/shard_map/all_gather | solution.py:125
  429.5 2.7 convert_reduce_fusion
  437.3 2.2 copy.36
  439.5 5.6 all-to-all-start.3
  445.7 123.2 %all-to-all-done.3 = bf16[8,128,1600]{1,2,0:T(8,128)(2,1)} async-done(((bf16[8,128,1600]{1,2,0:T(8,128)(2,1)}), bf16[8,128,1600]{1,2,0:T(8,128)(2,1)}, u32[]{:S(2)}, u32[]{:S(2)}) %all-to-all-start.3) | async-done | bytes 3276832 | tf_op jit(solution)/shard_map/all_to_all | solution.py:37
  568.9 2.6 fusion.42
  571.6 1.8 bitcast_convert_fusion.1
  573.4 59.6 %all_to_all.34 = bf16[8,128,1200]{1,2,0:T(8,128)(2,1)S(1)} all-to-all(bf16[8,128,1200]{1,2,0:T(8,128)(2,1)S(1)} %bitcast_convert_fusion.1), channel_id=1, replica_groups=mesh['row'=8,'col'=4] {'row'}, dimensions={0} | all-to-all | bytes 4915200 | tf_op jit(solution)/shard_map/all_to_all | solution.py:55
  633.9 2.4 convert_element_type.116
  636.3 10.9 %fusion.21 = bf16[1024,1200]{0,1:T(8,128)(2,1)} fusion(f32[150,8,8,128]{3,2,1,0:T(8,128)} %bitcast.94, bf16[1600,1200]{1,0:T(8,128)(2,1)} %all-gather.14.cloned.1.call-done, f32[1200]{0:T(1024)S(1)} %copy-done.12, pred[1024]{0:T(1024)(128)(4,1)S(1)} %fusion.64, bf16[1024,1600]{0,1:T(8,128)(2,1)S(1)} %copy-done.3, f32[1600]{0:T(1024)S(1)} %copy-done.8, ...), kind=kOutput, calls=%fused_computation.29 | convolution fusion | flops 3946905600 | bytes 14516416 | tf_op jit(solution)/shard_map/dot_general | solution.py:15
  (67 shorter events, 17.2 us)
Async XLA Ops:
  7.2 181.6 %copy-start = (bf16[4,16,1600]{2,1,0:T(8,128)(2,1)S(1)}, bf16[4,16,1600]{2,1,0:T(8,128)(2,1)}, u32[]{:S(2)}) copy-start(bf16[4,16,1600]{2,1,0:T(8,128)(2,1)} %param.30) | copy-start | bytes 614404
  7.2 38.3 %copy-start.7 = (f32[1600]{0:T(1024)S(1)}, f32[1600]{0:T(1024)}, u32[]{:S(2)}) copy-start(f32[1600]{0:T(1024)} %param.25) | copy-start | bytes 19204
  7.2 38.3 %copy-start.6 = (f32[1600]{0:T(1024)S(1)}, f32[1600]{0:T(1024)}, u32[]{:S(2)}) copy-start(f32[1600]{0:T(1024)} %param.26) | copy-start | bytes 19204
  7.2 34.4 %all-gather.6.cloned.1.call-start = ((), (), s32[]{:S(2)}) async-start(), calls=%async_computation.6 | async-start | bytes 4096000 | tf_op jit(solution)/shard_map/all_gather | solution.py:97
  7.9 325.6 %all-gather.8.cloned.1.call-start = ((), (), s32[]{:S(2)}) async-start(), calls=%async_computation.7 | async-start | bytes 5990400 | tf_op jit(solution)/shard_map/all_gather | solution.py:101
  10.5 41.2 %all-to-all-start.1 = ((bf16[8,1,4]{2,1,0:T(2,128)(2,1)}), bf16[8,1,4]{2,1,0:T(2,128)(2,1)S(1)}, u32[]{:S(2)}, u32[]{:S(2)}) async-start(bf16[8,1,4]{2,1,0:T(2,128)(2,1)} %copy.30), calls=%async_computation.1 | async-start | bytes 8192 | tf_op jit(solution)/shard_map/all_to_all | solution.py:38
  41.6 2.9 copy-start.2
  51.7 134.4 %all-to-all-start = ((bf16[8,128,1600]{1,2,0:T(8,128)(2,1)}), bf16[8,128,1600]{1,2,0:T(8,128)(2,1)}, u32[]{:S(2)}, u32[]{:S(2)}) async-start(bf16[8,128,1600]{1,2,0:T(8,128)(2,1)} %copy.29), calls=%async_computation | async-start | bytes 6553600 | tf_op jit(solution)/shard_map/all_to_all | solution.py:37
  57.2 291.3 %all-gather.10.cloned.1.call-start = ((), (), s32[]{:S(2)}) async-start(), calls=%async_computation.8 | async-start | bytes 5990400 | tf_op jit(solution)/shard_map/all_gather | solution.py:117
  57.9 339.8 %reduce-scatter.2.cloned.1.call-start = ((), (), s32[]{:S(2)}) async-start(), calls=%async_computation.9 | async-start | bytes 4096000 | tf_op jit(solution)/shard_map/reduce_scatter | solution.py:120
  330.6 3.0 copy-start.11
  348.4 10.9 %copy-start.13 = (s32[8]{0:T(128)S(1)}, s32[8]{0:T(128)}, u32[]{:S(2)}) copy-start(s32[8]{0:T(128)} %param.35) | copy-start | bytes 100
  348.4 49.2 %copy-start.4 = (bf16[1024,400]{0,1:T(8,128)(2,1)S(1)}, bf16[1024,400]{0,1:T(8,128)(2,1)}, u32[]{:S(2)}) copy-start(bf16[1024,400]{0,1:T(8,128)(2,1)} %param.18) | copy-start | bytes 2457604
  348.4 49.3 %copy-start.10 = (f32[400]{0:T(512)S(1)}, f32[400]{0:T(512)}, u32[]{:S(2)}) copy-start(f32[400]{0:T(512)} %param.22) | copy-start | bytes 4804
  359.3 70.2 %all-gather.12.cloned.1.call-start = ((), (), s32[]{:S(2)}) async-start(), calls=%async_computation.10 | async-start | bytes 4096000 | tf_op jit(solution)/shard_map/all_gather | solution.py:125
  359.4 73.9 %copy-start.8 = (f32[1600]{0:T(1024)S(1)}, f32[1600]{0:T(1024)}, u32[]{:S(2)}) copy-start(f32[1600]{0:T(1024)} %param.28) | copy-start | bytes 19204
  359.4 73.9 %copy-start.9 = (f32[1600]{0:T(1024)S(1)}, f32[1600]{0:T(1024)}, u32[]{:S(2)}) copy-start(f32[1600]{0:T(1024)} %param.27) | copy-start | bytes 19204
  429.5 2.9 copy-start.3
  439.5 129.5 %copy-start.5 = (bf16[4,16,1600]{2,1,0:T(8,128)(2,1)S(1)}, bf16[4,16,1600]{2,1,0:T(8,128)(2,1)}, u32[]{:S(2)}) copy-start(bf16[4,16,1600]{2,1,0:T(8,128)(2,1)} %param.31) | copy-start | bytes 614404
  439.5 129.5 %all-to-all-start.3 = ((bf16[8,128,1600]{1,2,0:T(8,128)(2,1)}), bf16[8,128,1600]{1,2,0:T(8,128)(2,1)}, u32[]{:S(2)}, u32[]{:S(2)}) async-start(bf16[8,128,1600]{1,2,0:T(8,128)(2,1)} %copy.36), calls=%async_computation.4 | async-start | bytes 6553600 | tf_op jit(solution)/shard_map/all_to_all | solution.py:37
  445.1 191.2 %all-gather.14.cloned.1.call-start = ((), (), s32[]{:S(2)}) async-start(), calls=%async_computation.11 | async-start | bytes 4608000 | tf_op jit(solution)/shard_map/all_gather | solution.py:130
  633.9 2.4 copy-start.12
  636.3 10.9 %copy-start.1 = (bf16[4,16,1600]{2,1,0:T(8,128)(2,1)S(1)}, bf16[4,16,1600]{2,1,0:T(8,128)(2,1)}, u32[]{:S(2)}) copy-start(bf16[4,16,1600]{2,1,0:T(8,128)(2,1)} %param.30) | copy-start | bytes 614404
Sparse Core Ops, SparseCore 0:
  9.6 31.9 all-gather.5
  43.8 147.3 all-gather.7
  193.4 137.5 all-gather.9
  359.4 38.2 reduce-scatter.1
  400.2 29.2 all-gather.11
  448.1 123.5 all-gather.13
where the time goes:
time: 655 us; the launch traced here: 654 us
  waiting for transfers between devices  345 us (53%)
  blocking collectives  198 us (30%)
  matrix products  50.8 us (8%)
  other arithmetic  19.1 us (3%)
  starting transfers between devices  18.6 us (3%)
  between operations  14.3 us (2%)
  local copies, waits for them, and re-layouts  7.61 us (1%)
    all_to_all x2, waiting for transfers between devices, adapter_update(): lax.all_to_all(outgoing, 'row', split_axis=0, concat_axis=0, tiled=True)  251 us
    all_to_all x2, blocking collectives, adapter_update(): lax.all_to_all(answer, 'row', split_axis=0, concat_axis=0, tiled=True)  198 us
    reduce_scatter x1, waiting for transfers between devices, per_device(): lax.psum_scatter(partial_value.astype(jnp.bfloat16), 'col', scatter_dimen...  38.2 us
    all_gather x1, waiting for transfers between devices, per_device(): gathered_next = lax.all_gather(h_out, 'col', axis=1, tiled=True)  29.4 us
    dot_general x2, matrix products, fold_rows(): return jnp.dot(operand, weight_piece, preferred_element_type=jnp.float32)  25.8 us
    all_gather x1, waiting for transfers between devices, per_device(): gathered = lax.all_gather(hidden, 'col', axis=1, tiled=True)  23.9 us
  transfers between devices with their start and end apart: 9, of which 5 were waited for; matrix products, arithmetic and copies ran while one was open for 7% of the time, Pallas kernels for 0%

commit v1 on v0

v1 whole, which is shorter than its diff:
```python
import functools
import jax
import jax.numpy as jnp
from jax import lax
from jax.experimental import pallas as pl
from jax.experimental.pallas import tpu as pltpu
from jax.sharding import PartitionSpec as P

MESH = pl.DeviceIdType.MESH


def gather_kernel(nw, nx, nz, *refs):
    ins, outs = refs[:nw], refs[nw:2 * nw]
    loc, zs, zr, xs, xr = refs[2 * nw:]
    row = lax.axis_index("row")
    z, x = row // nx, row % nx
    barrier = pltpu.get_barrier_semaphore()

    def peer(zz, xx):
        return {"row": zz * nx + xx}

    greet = [(z > 0, z - 1, x), (z < nz - 1, z + 1, x), (x > 0, z, x - 1), (x < nx - 1, z, x + 1)]
    total = jnp.int32(0)
    for ok, zz, xx in greet:
        total = total + ok.astype(jnp.int32)
        @pl.when(ok)
        def _():
            pl.semaphore_signal(barrier, inc=1, device_id=peer(zz, xx), device_id_type=MESH)
    pl.semaphore_wait(barrier, total)

    def copy(w, zz, xx, sem_s, sem_r, dz, dx, own=False):
        r = zz * nx + xx
        return pltpu.make_async_remote_copy(
            src_ref=ins[w] if own else outs[w].at[r], dst_ref=outs[w].at[r],
            send_sem=sem_s, recv_sem=sem_r, device_id=peer(dz, dx), device_id_type=MESH)

    pend = []

    def send(ok, cp):
        @pl.when(ok)
        def _():
            cp.start()
        pend.append((ok, cp))

    def recv(ok, cp):
        @pl.when(ok)
        def _():
            cp.wait_recv()

    def xsend(w, s, d, zz, ok, own):
        k = 2 * s + d
        send(ok & (x < nx - 1), copy(w, zz, x, xs.at[w, 0, 0, k], xr.at[w, 0, 0, k], z, x + 1, own))
        send(ok & (x > 0), copy(w, zz, x, xs.at[w, 0, 1, k], xr.at[w, 0, 1, k], z, x - 1, own))

    true = z >= 0
    locs = []
    for w in range(nw):
        c = pltpu.make_async_copy(ins[w], outs[w].at[row], loc.at[w])
        c.start()
        locs.append(c)
    for w in range(nw):
        for s in range(nz):
            if s > 0:
                recv(z - s >= 0, copy(w, z - s, x, zs.at[w, 0, s], zr.at[w, 0, s], z, x))
                recv(z + s < nz, copy(w, z + s, x, zs.at[w, 1, s], zr.at[w, 1, s], z, x))
            if s < nz - 1:
                send((z - s >= 0) & (z < nz - 1), copy(w, z - s, x, zs.at[w, 0, s + 1], zr.at[w, 0, s + 1], z + 1, x, s == 0))
                send((z + s < nz) & (z > 0), copy(w, z + s, x, zs.at[w, 1, s + 1], zr.at[w, 1, s + 1], z - 1, x, s == 0))
            for d in range(2 if s else 1):
                zz = z - s if d == 0 else z + s
                xsend(w, s, d, zz, (zz >= 0) & (zz < nz), s == 0)
            if s == 0 and w == 0:
                pass
    for w in range(nw):
        for t in range(1, nx):
            for s in range(nz):
                for d in range(2 if s else 1):
                    zz = z - s if d == 0 else z + s
                    ok = (zz >= 0) & (zz < nz)
                    k = 2 * s + d
                    for side in range(2):
                        xx = x - t if side == 0 else x + t
                        okx = ok & ((xx >= 0) & (xx < nx))
                        recv(okx, copy(w, zz, xx, xs.at[w, t - 1, side, k], xr.at[w, t - 1, side, k], z, x))
                        if t < nx - 1:
                            nxt = x + 1 if side == 0 else x - 1
                            send(okx & (nxt >= 0) & (nxt < nx),
                                 copy(w, zz, xx, xs.at[w, t, side, k], xr.at[w, t, side, k], z, nxt))
    for c in locs:
        c.wait()
    for ok, cp in pend:
        @pl.when(ok)
        def _():
            cp.wait_send()


def gather_weights(ws, nx, nz, cid=3):
    nw = len(ws)
    n = nx * nz
    D = pltpu.SemaphoreType.DMA
    return pl.pallas_call(
        functools.partial(gather_kernel, nw, nx, nz),
        out_shape=[jax.ShapeDtypeStruct((n,) + w.shape, w.dtype) for w in ws],
        in_specs=[pl.BlockSpec(memory_space=pl.ANY)] * nw,
        out_specs=[pl.BlockSpec(memory_space=pl.ANY)] * nw,
        scratch_shapes=[D((nw,)), D((nw, 2, nz)), D((nw, 2, nz)),
                        D((nw, nx - 1, 2, 2 * nz)), D((nw, nx - 1, 2, 2 * nz))],
        compiler_params=pltpu.CompilerParams(collective_id=cid, has_side_effects=True),
    )(*ws)


def layer_norm(values, gain_vec, shift_vec):
    row_mean = jnp.mean(values, axis=-1, keepdims=True)
    centred = values - row_mean
    variance = jnp.mean(centred * centred, axis=-1, keepdims=True)
    return centred * lax.rsqrt(variance + 1e-05) * gain_vec + shift_vec


def adapter_update(normalized, down_tile, up_tile):
    tiles = down_tile.shape[0]
    tiled = normalized.reshape(tiles, -1, normalized.shape[1])
    low = jnp.einsum("tid,tcd->tic", tiled, down_tile, preferred_element_type=jnp.float32)
    delta = jnp.einsum(
        "tic,tcf->tif", low.astype(jnp.bfloat16), up_tile, preferred_element_type=jnp.float32
    )
    return delta.astype(jnp.bfloat16).reshape(normalized.shape[0], -1).astype(jnp.float32)


def fetch_adapters(factors, adapter_storage_slot, tile_adapter_index):
    per_holder = factors[0].shape[0]
    rows = lax.axis_size("row")
    me = lax.axis_index("row")
    adapters = jnp.arange(adapter_storage_slot.shape[0], dtype=jnp.int32)

    def slots_of(indices):
        pick = (indices[..., None] == adapters).astype(jnp.int32)
        return jnp.sum(pick * adapter_storage_slot, axis=-1)

    every = slots_of(lax.all_gather(tile_adapter_index, "row", axis=0, tiled=False))
    mine = slots_of(tile_adapter_index)
    residents = me * per_holder + jnp.arange(per_holder, dtype=jnp.int32)
    wanted = jnp.any(every[:, :, None] == residents, axis=1).astype(jnp.bfloat16)
    stacked = jnp.concatenate(factors, axis=2)
    outgoing = jnp.einsum(
        "rf,fcd->rcd", wanted, stacked, preferred_element_type=jnp.float32
    ).astype(jnp.bfloat16)
    arrived = lax.all_to_all(outgoing, "row", split_axis=0, concat_axis=0, tiled=True)
    holder = (mine[:, None] // per_holder == jnp.arange(rows, dtype=jnp.int32)).astype(jnp.bfloat16)
    chosen = jnp.einsum(
        "to,ocd->tcd", holder, arrived, preferred_element_type=jnp.float32
    ).astype(jnp.bfloat16)
    widths = [f.shape[2] for f in factors]
    ends = [sum(widths[: i + 1]) for i in range(len(widths))]
    return [chosen[:, :, e - w : e] for w, e in zip(widths, ends)]


def per_device(
    nx,
    nz,
    hidden,
    up_weight,
    up_bias,
    down_weight,
    down_bias,
    query_key_value_weight,
    query_key_value_bias,
    block_norm_gain,
    block_norm_shift,
    following_norm_gain,
    following_norm_shift,
    up_down_factors,
    up_up_factors,
    query_key_value_down_factors,
    query_key_value_up_factors,
    adapter_storage_slot,
    tile_adapter_index,
    tile_token_rows,
):
    tok_rows = hidden.shape[0]
    tile_len = tok_rows // tile_adapter_index.shape[0]
    valid = (jnp.arange(tile_len, dtype=jnp.int32)[None, :] < tile_token_rows[:, None]).reshape(
        tok_rows, 1
    )
    up_down, up_up, qkv_down, qkv_up = fetch_adapters(
        [up_down_factors, up_up_factors, query_key_value_down_factors, query_key_value_up_factors],
        adapter_storage_slot,
        tile_adapter_index,
    )
    up_all, down_all, qkv_all = gather_weights(
        [up_weight, down_weight.T, query_key_value_weight], nx, nz
    )
    up_all, down_all, qkv_all = [w.reshape(-1, w.shape[2]) for w in (up_all, down_all, qkv_all)]
    gathered = lax.all_gather(hidden, "col", axis=1, tiled=True)
    normalized = layer_norm(
        gathered.astype(jnp.float32), block_norm_gain, block_norm_shift
    ).astype(jnp.bfloat16)
    up_projection = (
        jnp.dot(normalized, up_all, preferred_element_type=jnp.float32)
        + up_bias
        + adapter_update(normalized, up_down, up_up)
    )
    activated = jax.nn.gelu(up_projection, approximate=True).astype(jnp.bfloat16)
    partial_value = lax.dot_general(
        activated, down_all, (((1,), (1,)), ((), ())), preferred_element_type=jnp.float32
    )
    summed = lax.psum_scatter(
        partial_value.astype(jnp.bfloat16), "col", scatter_dimension=1, tiled=True
    ).astype(jnp.float32)
    mixed = hidden.astype(jnp.float32) + summed + down_bias
    h_out = jnp.where(valid, mixed, 0.0).astype(jnp.bfloat16)
    gathered_next = lax.all_gather(h_out, "col", axis=1, tiled=True)
    normalized_next = layer_norm(
        gathered_next.astype(jnp.float32), following_norm_gain, following_norm_shift
    ).astype(jnp.bfloat16)
    projected = (
        jnp.dot(normalized_next, qkv_all, preferred_element_type=jnp.float32)
        + query_key_value_bias
        + adapter_update(normalized_next, qkv_down, qkv_up)
    )
    qkv = jnp.where(valid, projected, 0.0).astype(jnp.bfloat16)
    return (h_out, qkv)


def solution(mesh):
    nx = max(mesh.shape["col"] // 2, 1)
    nz = mesh.shape["row"] // nx
    in_specs = (
        P("row", "col"),
        P("row", "col"),
        P("col"),
        P("col", "row"),
        P("col"),
        P("row", "col"),
        P("col"),
        P(),
        P(),
        P(),
        P(),
        P("row", None, None),
        P("row", None, "col"),
        P("row", None, None),
        P("row", None, "col"),
        P(),
        P("row"),
        P("row"),
    )
    return jax.shard_map(
        functools.partial(per_device, nx, nz),
        mesh=mesh,
        in_specs=in_specs,
        out_specs=(P("row", "col"), P("row", "col")),
        check_vma=False,
    )
```

time: 655 us -> 366 us (0.56)
  waiting for transfers between devices: 345 us -> 65.3 us
  Pallas kernels: 0 us -> 197 us
  blocking collectives: 198 us -> 13.1 us
  starting transfers between devices: 18.6 us -> 3.7 us
  other arithmetic: 19.1 us -> 11 us
    all_to_all x3 -> x1, waiting for transfers between devices: 251 us -> 0.01 us  [fetch_adapters(): lax.all_to_all(outgoing, 'row', split_axis=0, concat_axis=0, tiled=True)]
    all_to_all x2 -> x0, blocking collectives: 198 us -> none  [adapter_update(): lax.all_to_all(answer, 'row', split_axis=0, concat_axis=0, tiled=True)]
    pallas_call x0 -> x1, Pallas kernels: none -> 197 us  [gather_weights(): pl.pallas_call(functools.partial(gather_kernel, nw, nx, nz), out_shape=[j...]
    all_gather x1, waiting for transfers between devices: 23.9 us -> 0.01 us  [per_device(): gathered = lax.all_gather(hidden, 'col', axis=1, tiled=True)]
    all_to_all x3 -> x1, starting transfers between devices: 18.4 us -> 3.58 us  [fetch_adapters(): lax.all_to_all(outgoing, 'row', split_axis=0, concat_axis=0, tiled=True)]
    unnamed x0 -> x1, blocking collectives: none -> 13.1 us
    dot_general x12 -> x7, matrix products: 50.8 us -> 46.9 us  [the longest x1 13.2 us: per_device(): jnp.dot(normalized, up_all, preferred_element_type=jnp.float32) + up_bias]
  transfers between devices with their start and end apart: 9 -> 4, of which waited for: 5 -> 2; matrix products, arithmetic and copies ran while one was open for 7% -> 4% of each run, Pallas kernels for 0% -> 54%
where the time goes in v1:
time: 366 us; the launch traced here: 365 us
  Pallas kernels  197 us (54%)
  waiting for transfers between devices  65.3 us (18%)
  matrix products  46.9 us (13%)
  between operations  14.6 us (4%)
  local copies, waits for them, and re-layouts  13.6 us (4%)
  blocking collectives  13.1 us (4%)
  other arithmetic  11 us (3%)
  starting transfers between devices  3.7 us (1%)
    pallas_call x1, Pallas kernels, gather_weights(): pl.pallas_call(functools.partial(gather_kernel, nw, nx, nz), out_shape=[j...  197 us
    reduce_scatter x1, waiting for transfers between devices, per_device(): lax.psum_scatter(partial_value.astype(jnp.bfloat16), 'col', scatter_dimen...  37 us
    all_gather x1, waiting for transfers between devices, per_device(): gathered_next = lax.all_gather(h_out, 'col', axis=1, tiled=True)  27.6 us
    dot_general x1, matrix products, per_device(): jnp.dot(normalized, up_all, preferred_element_type=jnp.float32) + up_bias  13.2 us
    unnamed x1, blocking collectives  13.1 us
    dot_general x2, matrix products, adapter_update(): jnp.einsum('tic,tcf->tif', low.astype(jnp.bfloat16), up_tile, preferred_e...  11.9 us
    dot_general x1, matrix products, per_device(): jnp.dot(normalized_next, qkv_all, preferred_element_type=jnp.float32)  10.4 us
    dot_general x1, matrix products, per_device(): lax.dot_general(activated, down_all, (((1,), (1,)), ((), ())), preferred_...  10.2 us
  transfers between devices with their start and end apart: 4, of which 2 were waited for; matrix products, arithmetic and copies ran while one was open for 4% of the time, Pallas kernels for 54%

profile of v1, /device:TPU:0, one launch (start us, length us, event | category | flops | bytes accessed | tf_op | source)
XLA Modules:
  0.0 365.1 jit_solution(17466294422972838681)
XLA Ops:
  7.9 1.2 dynamic-slice
  10.7 13.1 %all-reduce = s32[64]{0:T(128)S(1)} all-reduce(s32[64]{0:T(128)S(1)} %dynamic-update-slice), channel_id=2, replica_groups=mesh['row'=8,'col'=4] {'row'}, use_global_device_ids=true, to_apply=%add | all-reduce | flops 64 | bytes 512
  23.8 1.0 copy.32
  24.8 1.0 copy.29
  25.8 1.0 copy.30
  26.9 1.0 copy.31
  27.9 1.3 concatenate.3
  29.2 1.0 select_reduce_fusion
  31.1 1.3 copy.33
  32.4 3.6 all-to-all-start
  36.1 196.9 %shard_map.185 = (bf16[8,200,1600]{2,1,0:T(8,128)(2,1)}, bf16[8,200,1600]{2,1,0:T(8,128)(2,1)}, bf16[8,200,1200]{2,1,0:T(8,128)(2,1)}) custom-call(bf16[200,1600]{1,0:T(8,128)(2,1)} %refs_0_.1, bf16[200,1600]{1,0:T(8,128)(2,1)} %bitcast.65, bf16[200,1200]{1,0:T(8,128)(2,1)} %refs_2_.1), custom_call_target="tpu_custom_call" | custom-call | tf_op jit(solution)/shard_map/pallas_call | solution.py:101
  233.9 1.1 copy-done.2
  235.0 1.2 fusion.59
  236.2 2.7 convert_reduce_fusion.1
  240.1 6.3 %convert_bitcast_fusion = f32[8,200,8,128]{3,2,1,0:T(8,128)} fusion(bf16[8,16,1600]{2,0,1:T(8,128)(2,1)} %get-tuple-element.9, bf16[8,16,1600]{2,0,1:T(8,128)(2,1)} %get-tuple-element.10, f32[1600]{0:T(1024)S(1)} %copy-done.4, f32[1600]{0:T(1024)S(1)} %copy-done.5, f32[1024]{0:T(1024)S(1)} %add_rsqrt_fusion.1, f32[1024]{0:T(1024)S(1)} %broadcast_multiply_fusion.1, ...), kind=kOutput, calls=%fused_computation.28 | convolution fusion | flops 117981184 | bytes 10670592 | tf_op jit(solution)/shard_map/tic,tcf->tif/dot_general | solution.py:123
  246.4 13.2 %fusion.19.clone.4 = bf16[1024,1600]{0,1:T(8,128)(2,1)S(1)} fusion(f32[8,200,8,128]{3,2,1,0:T(8,128)} %convert_bitcast_fusion, bf16[1600,1600]{1,0:T(8,128)(2,1)} %bitcast.67, f32[1600]{0:T(1024)S(1)} %copy-done.8, bf16[1024,1600]{0,1:T(8,128)(2,1)S(1)} %copy-done, f32[1600]{0:T(1024)S(1)} %copy-done.4, f32[1600]{0:T(1024)S(1)} %copy-done.5, ...), kind=kOutput, calls=%fused_computation.26.clone.clone.clone.1 | convolution fusion | flops 5270732800 | bytes 18254592 | tf_op jit(solution)/shard_map/dot_general | solution.py:198
  259.6 10.2 %convolution_convert_fusion.3 = bf16[1024,1600]{0,1:T(8,128)(2,1)} fusion(bf16[1600,1600]{1,0:T(8,128)(2,1)} %bitcast.66, bf16[1024,1600]{0,1:T(8,128)(2,1)S(1)} %fusion.19.clone.4), kind=kOutput, calls=%fused_computation.34 | convolution fusion | flops 5244518400 | bytes 11673600 | tf_op jit(solution)/shard_map/dot_general | solution.py:203
  270.0 37.0 %reduce-scatter.2.cloned.1.call-done = bf16[1024,400]{0,1:T(8,128)(2,1)} async-done(((bf16[1024,1600]{0,1:T(8,128)(2,1)}), bf16[1024,400]{0,1:T(8,128)(2,1)}) %reduce-scatter.2.cloned.1.call-update) | async-done | bytes 819216 | tf_op jit(solution)/shard_map/reduce_scatter | solution.py:206
  307.0 2.3 select_convert_fusion
  309.4 1.9 slice.19
  311.3 27.6 %all-gather.6.cloned.1.call-done = bf16[1024,1600]{0,1:T(8,128)(2,1)} async-done(((bf16[1024,400]{0,1:T(8,128)(2,1)}), bf16[1024,1600]{0,1:T(8,128)(2,1)}) %all-gather.6.cloned.1.call-update) | async-done | bytes 3276816 | tf_op jit(solution)/shard_map/all_gather | solution.py:211
  338.8 2.7 convert_reduce_fusion
  342.7 5.5 %convert_bitcast_fusion.1 = f32[8,150,8,128]{3,2,1,0:T(8,128)} fusion(bf16[8,16,1600]{2,0,1:T(8,128)(2,1)} %get-tuple-element.8, bf16[8,16,1200]{2,0,1:T(8,128)(2,1)} %slice.19, f32[1600]{0:T(1024)S(1)} %copy-done.9, f32[1600]{0:T(1024)S(1)} %copy-done.10, f32[1024]{0:T(1024)S(1)} %add_rsqrt_fusion, f32[1024]{0:T(1024)S(1)} %broadcast_multiply_fusion, ...), kind=kOutput, calls=%fused_computation.32 | convolution fusion | flops 104054784 | bytes 8929792 | tf_op jit(solution)/shard_map/tic,tcf->tif/dot_general | solution.py:123
  348.2 10.4 %fusion.21 = bf16[1024,1200]{0,1:T(8,128)(2,1)} fusion(f32[8,150,8,128]{3,2,1,0:T(8,128)} %convert_bitcast_fusion.1, bf16[1600,1200]{1,0:T(8,128)(2,1)} %bitcast.68, f32[1200]{0:T(1024)S(1)} %copy-done.11, pred[1024]{0:T(1024)(128)(4,1)S(1)} %fusion.45, bf16[1024,1600]{0,1:T(8,128)(2,1)S(1)} %copy-done.1, f32[1600]{0:T(1024)S(1)} %copy-done.9, ...), kind=kOutput, calls=%fused_computation.31 | convolution fusion | flops 3946905600 | bytes 14516416 | tf_op jit(solution)/shard_map/dot_general | solution.py:216
  (51 shorter events, 5.9 us)
Async XLA Ops:
  7.2 229.0 %all-gather.4.cloned.1.call-start = ((), (), s32[]{:S(2)}) async-start(), calls=%async_computation.2 | async-start | bytes 4096000 | tf_op jit(solution)/shard_map/all_gather | solution.py:193
  29.2 203.8 %copy-start.7 = (s32[32]{0:T(128)S(1)}, s32[32]{0:T(128)}, u32[]{:S(2)}) copy-start(s32[32]{0:T(128)} %param.33) | copy-start | bytes 388
  29.2 203.8 %copy-start.12 = (s32[8]{0:T(128)S(1)}, s32[8]{0:T(128)}, u32[]{:S(2)}) copy-start(s32[8]{0:T(128)} %param.34) | copy-start | bytes 100
  32.4 200.8 %all-to-all-start = ((bf16[8,16,6000]{2,1,0:T(8,128)(2,1)}), bf16[8,16,6000]{2,1,0:T(8,128)(2,1)S(1)}, u32[]{:S(2)}, u32[]{:S(2)}) async-start(bf16[8,16,6000]{2,1,0:T(8,128)(2,1)} %copy.33), calls=%async_computation | async-start | bytes 3080192 | tf_op jit(solution)/shard_map/all_to_all | solution.py:147
  36.0 271.0 %reduce-scatter.2.cloned.1.call-start = ((), (), s32[]{:S(2)}) async-start(), calls=%async_computation.3 | async-start | bytes 4096000 | tf_op jit(solution)/shard_map/reduce_scatter | solution.py:206
  233.8 1.1 copy-start.2
  235.0 5.0 %copy-start.4 = (f32[1600]{0:T(1024)S(1)}, f32[1600]{0:T(1024)}, u32[]{:S(2)}) copy-start(f32[1600]{0:T(1024)} %param.26) | copy-start | bytes 19204
  235.0 5.1 %copy-start.5 = (f32[1600]{0:T(1024)S(1)}, f32[1600]{0:T(1024)}, u32[]{:S(2)}) copy-start(f32[1600]{0:T(1024)} %param.25) | copy-start | bytes 19204
  236.2 2.9 copy-start
  240.0 6.4 %copy-start.8 = (f32[1600]{0:T(1024)S(1)}, f32[1600]{0:T(1024)}, u32[]{:S(2)}) copy-start(f32[1600]{0:T(1024)} %param.20) | copy-start | bytes 19204
  259.6 10.3 %copy-start.13 = (s32[8]{0:T(128)S(1)}, s32[8]{0:T(128)}, u32[]{:S(2)}) copy-start(s32[8]{0:T(128)} %param.35) | copy-start | bytes 100
  259.6 47.4 %copy-start.3 = (bf16[1024,400]{0,1:T(8,128)(2,1)S(1)}, bf16[1024,400]{0,1:T(8,128)(2,1)}, u32[]{:S(2)}) copy-start(bf16[1024,400]{0,1:T(8,128)(2,1)} %param.18) | copy-start | bytes 2457604
  259.6 47.4 %copy-start.6 = (f32[400]{0:T(512)S(1)}, f32[400]{0:T(512)}, u32[]{:S(2)}) copy-start(f32[400]{0:T(512)} %param.22) | copy-start | bytes 4804
  269.8 72.9 %copy-start.9 = (f32[1600]{0:T(1024)S(1)}, f32[1600]{0:T(1024)}, u32[]{:S(2)}) copy-start(f32[1600]{0:T(1024)} %param.28) | copy-start | bytes 19204
  269.8 72.8 %copy-start.10 = (f32[1600]{0:T(1024)S(1)}, f32[1600]{0:T(1024)}, u32[]{:S(2)}) copy-start(f32[1600]{0:T(1024)} %param.27) | copy-start | bytes 19204
  269.8 69.0 %all-gather.6.cloned.1.call-start = ((), (), s32[]{:S(2)}) async-start(), calls=%async_computation.4 | async-start | bytes 4096000 | tf_op jit(solution)/shard_map/all_gather | solution.py:211
  338.8 2.9 copy-start.1
  342.6 5.6 %copy-start.11 = (f32[1200]{0:T(1024)S(1)}, f32[1200]{0:T(1024)}, u32[]{:S(2)}) copy-start(f32[1200]{0:T(1024)} %param.24) | copy-start | bytes 14404
Sparse Core Ops, SparseCore 0:
  9.6 31.9 all-gather.3
  269.9 37.0 reduce-scatter.1
  309.5 29.2 all-gather.5

commit v2 on v1

v2 whole, which is shorter than its diff:
```python
import functools
import jax
import jax.numpy as jnp
from jax import lax
from jax.experimental import pallas as pl
from jax.experimental.pallas import tpu as pltpu
from jax.sharding import PartitionSpec as P

MESH = pl.DeviceIdType.MESH


def fused_kernel(
    nx, nz, nc, tile, chunk,
    holder, hid_in, up_in, dn_in, qk_in, fd_in, fu_in, fq_in, up_bias, dn_bias, qk_bias,
    gain1, shift1, gain2, shift2, valid,
    h_out, qkv_out,
    upw, dnw, qkw, hid, norm, act, part, rsb, nxt, fd, fu, fq, acc, feat,
    loc, zs, zr, xs, xr, hs, hr, ads, adr, rss, rsr, ags, agr,
):
    nr = nx * nz
    per = nr // nc
    rows, width = hid_in.shape
    piece = up_in.shape[0]
    model = width * nc
    chunks = rows // chunk
    row, col = lax.axis_index("row"), lax.axis_index("col")
    z, x = row // nx, row % nx
    barrier = pltpu.get_barrier_semaphore()

    @pl.loop(1, nr)
    def _(k):
        pl.semaphore_signal(barrier, inc=1, device_id={"row": lax.rem(row + k, nr)}, device_id_type=MESH)

    @pl.loop(1, nc)
    def _(k):
        pl.semaphore_signal(barrier, inc=1, device_id={"col": lax.rem(col + k, nc)}, device_id_type=MESH)

    pl.semaphore_wait(barrier, nr + nc - 2)
    ins, outs = (up_in, dn_in, qk_in), (upw, dnw, qkw)

    def copy(w, zz, xx, sem_s, sem_r, dz, dx, own=False):
        r = zz * nx + xx
        return pltpu.make_async_remote_copy(
            src_ref=ins[w] if own else outs[w].at[r], dst_ref=outs[w].at[r],
            send_sem=sem_s, recv_sem=sem_r,
            device_id={"row": dz * nx + dx}, device_id_type=MESH)

    pend = []

    def send(ok, cp):
        @pl.when(ok)
        def _():
            cp.start()
        pend.append((ok, cp))

    def recv(ok, cp):
        @pl.when(ok)
        def _():
            cp.wait_recv()

    def zstep(w, s):
        if s > 0:
            recv(z - s >= 0, copy(w, z - s, x, zs.at[w, 0, s], zr.at[w, 0, s], z, x))
            recv(z + s < nz, copy(w, z + s, x, zs.at[w, 1, s], zr.at[w, 1, s], z, x))
        if s < nz - 1:
            send((z - s >= 0) & (z < nz - 1), copy(w, z - s, x, zs.at[w, 0, s + 1], zr.at[w, 0, s + 1], z + 1, x, s == 0))
            send((z + s < nz) & (z > 0), copy(w, z + s, x, zs.at[w, 1, s + 1], zr.at[w, 1, s + 1], z - 1, x, s == 0))
        for d in range(2 if s else 1):
            zz = z - s if d == 0 else z + s
            ok = (zz >= 0) & (zz < nz)
            k = 2 * s + d
            send(ok & (x < nx - 1), copy(w, zz, x, xs.at[w, 0, 0, k], xr.at[w, 0, 0, k], z, x + 1, s == 0))
            send(ok & (x > 0), copy(w, zz, x, xs.at[w, 0, 1, k], xr.at[w, 0, 1, k], z, x - 1, s == 0))

    def xfinish(w):
        for t in range(1, nx):
            for s in range(nz):
                for d in range(2 if s else 1):
                    zz = z - s if d == 0 else z + s
                    ok = (zz >= 0) & (zz < nz)
                    k = 2 * s + d
                    for side in range(2):
                        xx = x - t if side == 0 else x + t
                        okx = ok & (xx >= 0) & (xx < nx)
                        recv(okx, copy(w, zz, xx, xs.at[w, t - 1, side, k], xr.at[w, t - 1, side, k], z, x))
                        if t < nx - 1:
                            to = x + 1 if side == 0 else x - 1
                            send(okx & (to >= 0) & (to < nx),
                                 copy(w, zz, xx, xs.at[w, t, side, k], xr.at[w, t, side, k], z, to))

    def col_copy(src, dst, ss, rs, k):
        return pltpu.make_async_remote_copy(
            src_ref=src, dst_ref=dst, send_sem=ss, recv_sem=rs,
            device_id={"col": lax.rem(col + k, nc)}, device_id_type=MESH)

    def hid_copy(k):
        return col_copy(hid_in, hid.at[col], hs.at[k], hr.at[k], k)

    def adapter_copy(i, k):
        src, dst = ((fd_in, fd), (fu_in, fu), (fq_in, fq))[i]
        to = lax.rem(row + k, nr)
        return pltpu.make_async_remote_copy(
            src_ref=src.at[to], dst_ref=dst.at[row], send_sem=ads.at[i, k], recv_sem=adr.at[i, k],
            device_id={"row": to}, device_id_type=MESH)

    def span(i):
        return pl.ds(pl.multiple_of(i * chunk, chunk), chunk)

    def rs_copy(i, k):
        to = lax.rem(col + k, nc)
        return col_copy(part.at[to, span(i)], rsb.at[col, span(i)], rss.at[i, k], rsr.at[i, k], k)

    def ag_copy(i, k):
        return col_copy(nxt.at[col, span(i)], nxt.at[col, span(i)], ags.at[i, k], agr.at[i, k], k)

    locs = [pltpu.make_async_copy(s, d.at[row], loc.at[i]) for i, (s, d) in enumerate(zip(ins, outs))]
    locs.append(pltpu.make_async_copy(hid_in, hid.at[col], loc.at[3]))
    for i, (s, d) in enumerate(((fd_in, fd), (fu_in, fu), (fq_in, fq))):
        locs.append(pltpu.make_async_copy(s.at[row], d.at[row], loc.at[4 + i]))
    zstep(0, 0)
    for k in range(1, nc):
        hid_copy(k).start()

    @pl.loop(1, nr)
    def _(k):
        for i in range(3):
            adapter_copy(i, k).start()

    for c in locs:
        c.start()

    def normalize(i, source, gain, shift):
        vals = [source[c, span(i), :].astype(jnp.float32) for c in range(nc)]
        mean = sum(jnp.sum(v, axis=1, keepdims=True) for v in vals) / model
        vals = [v - mean for v in vals]
        var = sum(jnp.sum(v * v, axis=1, keepdims=True) for v in vals) / model
        scale = lax.rsqrt(var + 1e-05)
        for c in range(nc):
            feat[...] = vals[c] * scale * gain[c] + shift[c]
            for j in range(per):
                norm[per * c + j, span(i), :] = feat[:, j * piece:(j + 1) * piece].astype(jnp.bfloat16)

    def project(i, weights, kind, ups, bias, out_width):
        total = jnp.zeros((chunk, out_width), jnp.float32)
        for r in range(nr):
            total = total + jnp.dot(norm[r, span(i), :], weights[r], preferred_element_type=jnp.float32)
        acc[:, :out_width] = total + bias[...]
        for j in range(chunk // tile):
            owner = holder[i * (chunk // tile) + j]
            downs = fd[owner, kind]
            up = ups[owner]
            here = pl.ds(pl.multiple_of(i * chunk + j * tile, tile), tile)
            low = jnp.zeros((tile, downs.shape[1]), jnp.float32)
            for r in range(nr):
                low = low + lax.dot_general(
                    norm[r, here, :], downs[r], (((1,), (1,)), ((), ())),
                    preferred_element_type=jnp.float32)
            delta = jnp.dot(low.astype(jnp.bfloat16), up, preferred_element_type=jnp.float32)
            acc[j * tile:(j + 1) * tile, :out_width] += delta.astype(jnp.bfloat16).astype(jnp.float32)

    def up_stage(i):
        project(i, upw, 0, fu, up_bias, act.shape[1])
        act[span(i), :] = jax.nn.gelu(acc[:, :act.shape[1]], approximate=True).astype(jnp.bfloat16)

    def down_stage(i):
        for c in range(nc):
            for j in range(per):
                feat[:, j * piece:(j + 1) * piece] = lax.dot_general(
                    act[span(i), :], dnw[per * c + j], (((1,), (1,)), ((), ())),
                    preferred_element_type=jnp.float32)
            part[c, span(i), :] = feat[...].astype(jnp.bfloat16)
        for k in range(1, nc):
            rs_copy(i, k).start()

    def mix_stage(i):
        for k in range(1, nc):
            rs_copy(i, k).wait_recv()
        total = part[col, span(i), :].astype(jnp.float32)
        for k in range(1, nc):
            total = total + rsb[lax.rem(col + k, nc), span(i), :].astype(jnp.float32)
        mixed = hid[col, span(i), :].astype(jnp.float32) + total + dn_bias[...]
        new = jnp.where(valid[span(i), :] > 0, mixed, 0.0).astype(jnp.bfloat16)
        h_out[span(i), :] = new
        nxt[col, span(i), :] = new
        for k in range(1, nc):
            ag_copy(i, k).start()

    def qkv_stage(i):
        for k in range(1, nc):
            ag_copy(i, k).wait_recv()
        normalize(i, nxt, gain2, shift2)
        wide = qkv_out.shape[1]
        project(i, qkw, 1, fq, qk_bias, wide)
        qkv_out[span(i), :] = jnp.where(valid[span(i), :] > 0, acc[:, :wide], 0.0).astype(jnp.bfloat16)

    def every(first, last, stage):
        lax.fori_loop(first, last, lambda i, c: (stage(i), c)[1], 0)

    for s in range(1, nz - 1):
        zstep(0, s)
    locs[3].wait()
    for k in range(1, nc):
        hid_copy(k).wait_recv()
    every(0, chunks, lambda i: normalize(i, hid, gain1, shift1))
    zstep(0, nz - 1)
    zstep(1, 0)

    @pl.loop(1, nr)
    def _(k):
        for i in range(3):
            adapter_copy(i, k).wait_recv()

    for c in locs[:3] + locs[4:]:
        c.wait()
    zstep(1, 1)
    xfinish(0)
    every(0, chunks // 2, up_stage)
    for s in range(2, nz):
        zstep(1, s)
    zstep(2, 0)
    every(chunks // 2, chunks, up_stage)
    for s in range(1, nz):
        zstep(2, s)
    xfinish(1)
    every(0, chunks, down_stage)
    every(0, chunks, mix_stage)
    xfinish(2)
    every(0, chunks, qkv_stage)

    for ok, cp in pend:
        @pl.when(ok)
        def _():
            cp.wait_send()
    for k in range(1, nc):
        hid_copy(k).wait_send()

    @pl.loop(1, nr)
    def _(k):
        for i in range(3):
            adapter_copy(i, k).wait_send()

    @pl.loop(0, chunks)
    def _(i):
        for k in range(1, nc):
            rs_copy(i, k).wait_send()
            ag_copy(i, k).wait_send()


def fetch_adapters(factors, adapter_storage_slot, tile_adapter_index):
    per_holder = factors[0].shape[0]
    rows = lax.axis_size("row")
    me = lax.axis_index("row")
    adapters = jnp.arange(adapter_storage_slot.shape[0], dtype=jnp.int32)

    def slots_of(indices):
        pick = (indices[..., None] == adapters).astype(jnp.int32)
        return jnp.sum(pick * adapter_storage_slot, axis=-1)

    every = slots_of(lax.all_gather(tile_adapter_index, "row", axis=0, tiled=False))
    mine = slots_of(tile_adapter_index)
    residents = me * per_holder + jnp.arange(per_holder, dtype=jnp.int32)
    wanted = jnp.any(every[:, :, None] == residents, axis=1).astype(jnp.bfloat16)
    picked = [
        jnp.einsum("rf,fcd->rcd", wanted, f, preferred_element_type=jnp.float32).astype(jnp.bfloat16)
        for f in factors
    ]
    return picked, mine // per_holder


def per_device(
    nx,
    nz,
    hidden,
    up_weight,
    up_bias,
    down_weight,
    down_bias,
    query_key_value_weight,
    query_key_value_bias,
    block_norm_gain,
    block_norm_shift,
    following_norm_gain,
    following_norm_shift,
    up_down_factors,
    up_up_factors,
    query_key_value_down_factors,
    query_key_value_up_factors,
    adapter_storage_slot,
    tile_adapter_index,
    tile_token_rows,
):
    tok_rows, width = hidden.shape
    tile_len = tok_rows // tile_adapter_index.shape[0]
    nr, nc = nx * nz, lax.axis_size("col")
    piece = up_weight.shape[0]
    valid = (jnp.arange(tile_len, dtype=jnp.int32)[None, :] < tile_token_rows[:, None]).reshape(
        tok_rows, 1
    )
    (up_down, up_up, qkv_down, qkv_up), holder = fetch_adapters(
        [up_down_factors, up_up_factors, query_key_value_down_factors, query_key_value_up_factors],
        adapter_storage_slot,
        tile_adapter_index,
    )
    rank = up_down.shape[1]
    downs = jnp.stack([up_down, qkv_down], axis=1).reshape(nr, 2, rank, nr, piece)
    downs = downs.transpose(0, 1, 3, 2, 4)
    chunk = min(2 * tile_len, tok_rows)
    chunks = tok_rows // chunk
    hu, qc = up_weight.shape[1], query_key_value_weight.shape[1]
    dma = pltpu.SemaphoreType.DMA
    bf, f32 = jnp.bfloat16, jnp.float32
    anywhere = pl.BlockSpec(memory_space=pl.ANY)
    vmem = pl.BlockSpec(memory_space=pltpu.VMEM)
    return tuple(pl.pallas_call(
        functools.partial(fused_kernel, nx, nz, nc, tile_len, chunk),
        out_shape=[
            jax.ShapeDtypeStruct((tok_rows, width), bf),
            jax.ShapeDtypeStruct((tok_rows, qc), bf),
        ],
        in_specs=[pl.BlockSpec(memory_space=pltpu.SMEM)] + [anywhere] * 7 + [vmem] * 8,
        out_specs=[vmem, vmem],
        scratch_shapes=[
            pltpu.VMEM((nr, piece, hu), bf),
            pltpu.VMEM((nr, piece, hu), bf),
            pltpu.VMEM((nr, piece, qc), bf),
            pltpu.VMEM((nc, tok_rows, width), bf),
            pltpu.VMEM((nr, tok_rows, piece), bf),
            pltpu.VMEM((tok_rows, hu), bf),
            pltpu.VMEM((nc, tok_rows, width), bf),
            pltpu.VMEM((nc, tok_rows, width), bf),
            pltpu.VMEM((nc, tok_rows, width), bf),
            pltpu.VMEM(downs.shape, bf),
            pltpu.VMEM(up_up.shape, bf),
            pltpu.VMEM(qkv_up.shape, bf),
            pltpu.VMEM((chunk, max(hu, qc)), f32),
            pltpu.VMEM((chunk, width), f32),
            dma((7,)),
            dma((3, 2, nz)), dma((3, 2, nz)),
            dma((3, nx - 1, 2, 2 * nz)), dma((3, nx - 1, 2, 2 * nz)),
            dma((nc,)), dma((nc,)),
            dma((3, nr)), dma((3, nr)),
            dma((chunks, nc)), dma((chunks, nc)),
            dma((chunks, nc)), dma((chunks, nc)),
        ],
        compiler_params=pltpu.CompilerParams(
            collective_id=5, has_side_effects=True, vmem_limit_bytes=62 * 1024 * 1024
        ),
    )(
        holder, hidden, up_weight, down_weight.T, query_key_value_weight, downs, up_up, qkv_up,
        up_bias[None], down_bias[None], query_key_value_bias[None],
        block_norm_gain.reshape(nc, 1, width), block_norm_shift.reshape(nc, 1, width),
        following_norm_gain.reshape(nc, 1, width), following_norm_shift.reshape(nc, 1, width),
        valid.astype(jnp.int32),
    ))


def solution(mesh):
    nx = max(mesh.shape["col"] // 2, 1)
    nz = mesh.shape["row"] // nx
    in_specs = (
        P("row", "col"),
        P("row", "col"),
        P("col"),
        P("col", "row"),
        P("col"),
        P("row", "col"),
        P("col"),
        P(),
        P(),
        P(),
        P(),
        P("row", None, None),
        P("row", None, "col"),
        P("row", None, None),
        P("row", None, "col"),
        P(),
        P("row"),
        P("row"),
    )
    return jax.shard_map(
        functools.partial(per_device, nx, nz),
        mesh=mesh,
        in_specs=in_specs,
        out_specs=(P("row", "col"), P("row", "col")),
        check_vma=False,
    )
```

time: 366 us -> 303 us (0.83); the launches traced: 365 us -> 298 us
  waiting for transfers between devices: 65.3 us -> 0 us
  Pallas kernels: 197 us -> 254 us
  matrix products: 46.9 us -> 2.19 us
  between operations: 14.6 us -> 1.41 us
  local copies, waits for them, and re-layouts: 13.6 us -> 22.9 us
  other arithmetic: 11 us -> 4.51 us
  starting transfers between devices: 3.7 us -> 0 us
    pallas_call x1, Pallas kernels: 197 us -> 254 us  [per_device(): pl.pallas_call(functools.partial(fused_kernel, nx, nz, nc, tile_len, chun...]
    dot_general x7 -> x4, matrix products: 46.9 us -> 2.19 us  [fetch_adapters(): jnp.einsum('rf,fcd->rcd', wanted, f, preferred_element_type=jnp.float32)]
    reduce_scatter x1 -> x0, waiting for transfers between devices: 37 us -> none  [per_device(): lax.psum_scatter(partial_value.astype(jnp.bfloat16), 'col', scatter_dimen...]
    all_gather x2 -> x0, waiting for transfers between devices: 27.6 us -> none  [the longest x1 27.6 us: per_device(): gathered_next = lax.all_gather(h_out, 'col', axis=1, tiled=True)]
    reduce_sum x4 -> x0, other arithmetic: 7.19 us -> none  [the longest x2 5.37 us: layer_norm(): row_mean = jnp.mean(values, axis=-1, keepdims=True)]
    pallas_call x0 -> x2, local copies, waits for them, and re-layouts: none -> 6.52 us  [per_device(): pl.pallas_call(functools.partial(fused_kernel, nx, nz, nc, tile_len, chun...]
    reshape x0 -> x4, local copies, waits for them, and re-layouts: none -> 5.48 us  [the longest x1 1.37 us: per_device(): block_norm_shift.reshape(nc, 1, width)]
    unnamed x35 -> x12, local copies, waits for them, and re-layouts: 7.78 us -> 3.45 us
  transfers between devices with their start and end apart: 4 -> 0, of which waited for: 2 -> 0; matrix products, arithmetic and copies ran while one was open for 4% -> 0% of each run, Pallas kernels for 54% -> 0%
where the time goes in v2:
time: 303 us; the launch traced here: 298 us
  Pallas kernels  254 us (84%)
  local copies, waits for them, and re-layouts  22.9 us (8%)
  blocking collectives  13.1 us (4%)
  other arithmetic  4.51 us (1%)
    pallas_call x1, Pallas kernels, per_device(): pl.pallas_call(functools.partial(fused_kernel, nx, nz, nc, tile_len, chun...  254 us
    unnamed x1, blocking collectives  13.1 us
    pallas_call x2, local copies, waits for them, and re-layouts, per_device(): pl.pallas_call(functools.partial(fused_kernel, nx, nz, nc, tile_len, chun...  6.52 us

profile of v2, /device:TPU:0, one launch (start us, length us, event | category | flops | bytes accessed | tf_op | source)
XLA Modules:
  0.0 297.9 jit_solution(7510667881195372973)
XLA Ops:
  0.7 1.3 dynamic-slice
  2.6 0.9 select_reduce_fusion.1
  3.5 0.6 and_select_fusion.holder
  4.1 0.8 dynamic-update-slice
  4.9 13.1 %all-reduce = s32[64]{0:T(128)S(1)} all-reduce(s32[64]{0:T(128)S(1)} %dynamic-update-slice), channel_id=2, replica_groups=mesh['row'=8,'col'=4] {'row'}, use_global_device_ids=true, to_apply=%add | all-reduce | flops 64 | bytes 512
  18.1 0.9 select_reduce_fusion
  19.2 0.7 fusion.6
  20.0 1.3 broadcast_in_dim.8.qk_bias
  21.2 1.3 broadcast_in_dim.6.up_bias
  22.5 1.4 reshape.59.gain1
  23.9 1.4 reshape.60.shift1
  25.3 1.4 reshape.61.gain2
  26.7 1.4 reshape.62.shift2
  28.0 1.2 fusion.4
  29.3 0.8 copy.72.fq_in
  30.4 0.8 reshape.72
  31.8 0.8 copy.71.fu_in
  33.0 0.8 reshape.71
  34.1 1.2 maximum_bitcast_fusion.fd_in
  35.2 1.0 copy.54.valid
  36.3 1.3 copy.53.hid_in
  37.6 253.8 %shard_map.185 = (bf16[1024,400]{1,0:T(8,128)(2,1)}, bf16[1024,1200]{1,0:T(8,128)(2,1)}) custom-call(s32[8]{0:T(128)} %and_select_fusion.holder, bf16[1024,400]{1,0:T(8,128)(2,1)} %copy.53.hid_in, bf16[200,1600]{1,0:T(8,128)(2,1)} %up_in.1, bf16[200,1600]{1,0:T(8,128)(2,1)} %bitcast.19, bf16[200,1200]{1,0:T(8,128)(2,1)} %qk_in.1, ...), custom_call_target="tpu_custom_call" | custom-call | tf_op jit(solution)/shard_map/pallas_call | solution.py:314
  291.3 2.2 copy.55
  293.5 4.3 %copy.56 = bf16[1024,1200]{0,1:T(8,128)(2,1)} copy(bf16[1024,1200]{1,0:T(8,128)(2,1)} %get-tuple-element.7) | data formatting | bytes 4915200 | tf_op jit(solution)/shard_map/pallas_call | solution.py:314
  (17 shorter events, 1.9 us)
Async XLA Ops:
  0.6 29.4 %copy-start = (bf16[4,16,1600]{2,1,0:T(8,128)(2,1)S(1)}, bf16[4,16,1600]{2,1,0:T(8,128)(2,1)}, u32[]{:S(2)}) copy-start(bf16[4,16,1600]{2,1,0:T(8,128)(2,1)} %param.31) | copy-start | bytes 614404
  0.6 30.9 %copy-start.2 = (bf16[4,16,1600]{2,1,0:T(8,128)(2,1)S(1)}, bf16[4,16,1600]{2,1,0:T(8,128)(2,1)}, u32[]{:S(2)}) copy-start(bf16[4,16,1600]{2,1,0:T(8,128)(2,1)} %param.30) | copy-start | bytes 614404
  28.0 4.6 %copy-start.3 = (bf16[4,16,1600]{2,1,0:T(8,128)(2,1)S(1)}, bf16[4,16,1600]{2,1,0:T(8,128)(2,1)}, u32[]{:S(2)}) copy-start(bf16[4,16,1600]{2,1,0:T(8,128)(2,1)} %param.29) | copy-start | bytes 614404
  32.6 3.6 %copy-start.1 = (bf16[1024,400]{0,1:T(8,128)(2,1)S(1)}, bf16[1024,400]{0,1:T(8,128)(2,1)}, u32[]{:S(2)}) copy-start(bf16[1024,400]{0,1:T(8,128)(2,1)} %param.18) | copy-start | bytes 2457604

commit v3 on v2

--- a/solution.py
+++ b/solution.py
@@ -12,7 +12,7 @@
 def fused_kernel(
     nx, nz, nc, tile, chunk,
     holder, hid_in, up_in, dn_in, qk_in, fd_in, fu_in, fq_in, up_bias, dn_bias, qk_bias,
-    gain1, shift1, gain2, shift2, valid,
+    norms, valid,
     h_out, qkv_out,
     upw, dnw, qkw, hid, norm, act, part, rsb, nxt, fd, fu, fq, acc, feat,
     loc, zs, zr, xs, xr, hs, hr, ads, adr, rss, rsr, ags, agr,
@@ -58,19 +58,25 @@
         def _():
             cp.wait_recv()
 
-    def zstep(w, s):
+    def zpart(w, s):
         if s > 0:
             recv(z - s >= 0, copy(w, z - s, x, zs.at[w, 0, s], zr.at[w, 0, s], z, x))
             recv(z + s < nz, copy(w, z + s, x, zs.at[w, 1, s], zr.at[w, 1, s], z, x))
         if s < nz - 1:
             send((z - s >= 0) & (z < nz - 1), copy(w, z - s, x, zs.at[w, 0, s + 1], zr.at[w, 0, s + 1], z + 1, x, s == 0))
             send((z + s < nz) & (z > 0), copy(w, z + s, x, zs.at[w, 1, s + 1], zr.at[w, 1, s + 1], z - 1, x, s == 0))
+
+    def xpart(w, s):
         for d in range(2 if s else 1):
             zz = z - s if d == 0 else z + s
             ok = (zz >= 0) & (zz < nz)
             k = 2 * s + d
             send(ok & (x < nx - 1), copy(w, zz, x, xs.at[w, 0, 0, k], xr.at[w, 0, 0, k], z, x + 1, s == 0))
             send(ok & (x > 0), copy(w, zz, x, xs.at[w, 0, 1, k], xr.at[w, 0, 1, k], z, x - 1, s == 0))
+
+    def zstep(w, s):
+        zpart(w, s)
+        xpart(w, s)
 
     def xfinish(w):
         for t in range(1, nx):
@@ -129,14 +135,14 @@
     for c in locs:
         c.start()
 
-    def normalize(i, source, gain, shift):
+    def normalize(i, source, base):
         vals = [source[c, span(i), :].astype(jnp.float32) for c in range(nc)]
         mean = sum(jnp.sum(v, axis=1, keepdims=True) for v in vals) / model
         vals = [v - mean for v in vals]
         var = sum(jnp.sum(v * v, axis=1, keepdims=True) for v in vals) / model
         scale = lax.rsqrt(var + 1e-05)
         for c in range(nc):
-            feat[...] = vals[c] * scale * gain[c] + shift[c]
+            feat[...] = vals[c] * scale * norms[base + c] + norms[base + nc + c]
             for j in range(per):
                 norm[per * c + j, span(i), :] = feat[:, j * piece:(j + 1) * piece].astype(jnp.bfloat16)
 
@@ -188,7 +194,7 @@
     def qkv_stage(i):
         for k in range(1, nc):
             ag_copy(i, k).wait_recv()
-        normalize(i, nxt, gain2, shift2)
+        normalize(i, nxt, 2 * nc)
         wide = qkv_out.shape[1]
         project(i, qkw, 1, fq, qk_bias, wide)
         qkv_out[span(i), :] = jnp.where(valid[span(i), :] > 0, acc[:, :wide], 0.0).astype(jnp.bfloat16)
@@ -196,14 +202,17 @@
     def every(first, last, stage):
         lax.fori_loop(first, last, lambda i, c: (stage(i), c)[1], 0)
 
-    for s in range(1, nz - 1):
+    for s in range(1, nz):
         zstep(0, s)
+        if s == 1:
+            zpart(1, 0)
+    xpart(1, 0)
+    zpart(1, 1)
+    zpart(2, 0)
     locs[3].wait()
     for k in range(1, nc):
         hid_copy(k).wait_recv()
-    every(0, chunks, lambda i: normalize(i, hid, gain1, shift1))
-    zstep(0, nz - 1)
-    zstep(1, 0)
+    every(0, chunks, lambda i: normalize(i, hid, 0))
 
     @pl.loop(1, nr)
     def _(k):
@@ -212,17 +221,21 @@
 
     for c in locs[:3] + locs[4:]:
         c.wait()
-    zstep(1, 1)
     xfinish(0)
+    xpart(1, 1)
     every(0, chunks // 2, up_stage)
     for s in range(2, nz):
         zstep(1, s)
-    zstep(2, 0)
     every(chunks // 2, chunks, up_stage)
-    for s in range(1, nz):
-        zstep(2, s)
+    for s in range(1, nz - 1):
+        zpart(2, s)
+    xpart(2, 0)
     xfinish(1)
-    every(0, chunks, down_stage)
+    for s in range(1, nz - 1):
+        xpart(2, s)
+    every(0, chunks // 2, down_stage)
+    zstep(2, nz - 1)
+    every(chunks // 2, chunks, down_stage)
     every(0, chunks, mix_stage)
     xfinish(2)
     every(0, chunks, qkv_stage)
@@ -317,7 +330,7 @@
             jax.ShapeDtypeStruct((tok_rows, width), bf),
             jax.ShapeDtypeStruct((tok_rows, qc), bf),
         ],
-        in_specs=[pl.BlockSpec(memory_space=pltpu.SMEM)] + [anywhere] * 7 + [vmem] * 8,
+        in_specs=[pl.BlockSpec(memory_space=pltpu.SMEM)] + [anywhere] * 7 + [vmem] * 5,
         out_specs=[vmem, vmem],
         scratch_shapes=[
             pltpu.VMEM((nr, piece, hu), bf),
@@ -348,8 +361,9 @@
     )(
         holder, hidden, up_weight, down_weight.T, query_key_value_weight, downs, up_up, qkv_up,
         up_bias[None], down_bias[None], query_key_value_bias[None],
-        block_norm_gain.reshape(nc, 1, width), block_norm_shift.reshape(nc, 1, width),
-        following_norm_gain.reshape(nc, 1, width), following_norm_shift.reshape(nc, 1, width),
+        jnp.concatenate(
+            [block_norm_gain, block_norm_shift, following_norm_gain, following_norm_shift]
+        ).reshape(4 * nc, 1, width),
         valid.astype(jnp.int32),
     ))
 

time: 303 us -> 305 us (level)
  Pallas kernels: 254 us -> 259 us
    reshape x4 -> x0, local copies, waits for them, and re-layouts: 5.48 us -> none  [the longest x1 1.37 us: per_device(): block_norm_shift.reshape(nc, 1, width)]
    pallas_call x1, Pallas kernels: 254 us -> 259 us  [per_device(): pl.pallas_call(functools.partial(fused_kernel, nx, nz, nc, tile_len, chun...]
    concatenate x0 -> x4, local copies, waits for them, and re-layouts: none -> 3.11 us  [per_device(): jnp.concatenate([block_norm_gain, block_norm_shift, following_norm_gain,...]
where the time goes in v3:
time: 305 us; the launch traced here: 301 us
  Pallas kernels  259 us (85%)
  local copies, waits for them, and re-layouts  20.6 us (7%)
  blocking collectives  13.1 us (4%)
  other arithmetic  5.08 us (2%)
    pallas_call x1, Pallas kernels, per_device(): pl.pallas_call(functools.partial(fused_kernel, nx, nz, nc, tile_len, chun...  259 us
    unnamed x1, blocking collectives  13.1 us
    pallas_call x2, local copies, waits for them, and re-layouts, per_device(): pl.pallas_call(functools.partial(fused_kernel, nx, nz, nc, tile_len, chun...  6.52 us

profile of v3, /device:TPU:0, one launch (start us, length us, event | category | flops | bytes accessed | tf_op | source)
XLA Modules:
  0.0 301.5 jit_solution(17785149114118424723)
XLA Ops:
  0.7 1.3 dynamic-slice
  2.6 0.9 select_reduce_fusion.1
  4.0 0.8 dynamic-update-slice
  4.9 13.1 %all-reduce = s32[64]{0:T(128)S(1)} all-reduce(s32[64]{0:T(128)S(1)} %dynamic-update-slice), channel_id=2, replica_groups=mesh['row'=8,'col'=4] {'row'}, use_global_device_ids=true, to_apply=%add | all-reduce | flops 64 | bytes 512
  18.0 0.9 select_reduce_fusion
  19.2 0.7 fusion.6
  19.9 1.3 broadcast_in_dim.8.qk_bias
  21.2 1.3 broadcast_in_dim.6.up_bias
  22.5 0.8 concatenate.13
  23.2 0.8 concatenate.14
  24.0 0.8 concatenate.15
  24.8 0.8 concatenate.16
  25.6 0.6 pad_maximum_fusion.norms
  26.2 1.2 fusion.4
  27.5 0.8 copy.72.fq_in
  28.6 0.8 reshape.61
  30.0 0.8 copy.71.fu_in
  31.2 0.8 reshape.60
  32.3 1.2 maximum_bitcast_fusion.fd_in
  33.5 1.0 copy.54.valid
  34.5 1.3 copy.53.hid_in
  35.8 259.2 %shard_map.185 = (bf16[1024,400]{1,0:T(8,128)(2,1)}, bf16[1024,1200]{1,0:T(8,128)(2,1)}) custom-call(s32[8]{0:T(128)} %and_select_fusion.holder, bf16[1024,400]{1,0:T(8,128)(2,1)} %copy.53.hid_in, bf16[200,1600]{1,0:T(8,128)(2,1)} %up_in.1, bf16[200,1600]{1,0:T(8,128)(2,1)} %bitcast.19, bf16[200,1200]{1,0:T(8,128)(2,1)} %qk_in.1, ...), custom_call_target="tpu_custom_call" | custom-call | tf_op jit(solution)/shard_map/pallas_call | solution.py:327
  295.0 2.2 copy.55
  297.1 4.3 %copy.56 = bf16[1024,1200]{0,1:T(8,128)(2,1)} copy(bf16[1024,1200]{1,0:T(8,128)(2,1)} %get-tuple-element.7) | data formatting | bytes 4915200 | tf_op jit(solution)/shard_map/pallas_call | solution.py:327
  (18 shorter events, 2.4 us)
Async XLA Ops:
  0.6 27.6 %copy-start = (bf16[4,16,1600]{2,1,0:T(8,128)(2,1)S(1)}, bf16[4,16,1600]{2,1,0:T(8,128)(2,1)}, u32[]{:S(2)}) copy-start(bf16[4,16,1600]{2,1,0:T(8,128)(2,1)} %param.31) | copy-start | bytes 614404
  0.6 29.1 %copy-start.2 = (bf16[4,16,1600]{2,1,0:T(8,128)(2,1)S(1)}, bf16[4,16,1600]{2,1,0:T(8,128)(2,1)}, u32[]{:S(2)}) copy-start(bf16[4,16,1600]{2,1,0:T(8,128)(2,1)} %param.30) | copy-start | bytes 614404
  26.2 4.6 %copy-start.3 = (bf16[4,16,1600]{2,1,0:T(8,128)(2,1)S(1)}, bf16[4,16,1600]{2,1,0:T(8,128)(2,1)}, u32[]{:S(2)}) copy-start(bf16[4,16,1600]{2,1,0:T(8,128)(2,1)} %param.29) | copy-start | bytes 614404
  30.8 3.6 %copy-start.1 = (bf16[1024,400]{0,1:T(8,128)(2,1)S(1)}, bf16[1024,400]{0,1:T(8,128)(2,1)}, u32[]{:S(2)}) copy-start(bf16[1024,400]{0,1:T(8,128)(2,1)} %param.18) | copy-start | bytes 2457604
